TPU v7x, 32 devices: a whole 2x2x4 slice. The times are simulated.
32 devices in a mesh: dom: 8 (over z, y), tile: 4 (over x, core).
Axes of the slice: x: 2, y: 2, z: 4, core: 2. Of those that a mesh axis runs over, the one named last changes fastest.
Arguments:
- embeddings: float32 [2048, 256], P(('dom', 'tile')), may hold values from -1.5 to 1.5
- adagrad_state: float32 [2048], P(('dom', 'tile')), may hold values from 0.1 to 2
- offsets: int32 [2], replicated, may hold values from 1 to 7, as said below
- lhs_rows: int32 [8, 2, 96, 128], P('dom', None, 'tile'), may hold values from 0 to 255
- rhs_rows: int32 [8, 2, 96, 128], P('dom', None, 'tile'), may hold values from 0 to 255
- neg_blocks: int32 [8, 2, 96], P('dom', None, 'tile'), may hold values from 0 to 1
- tile_counts: int32 [8, 2], P('dom'), may hold values from 12 to 72, as said below
Outputs:
- new_embeddings: float32 [2048, 256], P(('dom', 'tile'))
- new_state: float32 [2048], P(('dom', 'tile'))
Inputs may be any that keep to these rules, and one draw needn't show every extreme that they name: `offsets`: in one round of every draw the offset has all bits of a partition number set. `tile_counts`: in every round some bucket has exactly 72 live tiles.
All inputs are finite; a program needn't handle non-finite values.
Results may differ from a plain program's by a relative error of at most 0.007.
Values may be sent and summed in bfloat16 or wider, within the bound.
A program may use at most 64 MiB of HBM per device.

v0:
```python
import functools

import jax
import jax.numpy as jnp
from jax import lax
from jax.experimental import pallas as pl
from jax.experimental.pallas import tpu as pltpu
from jax.sharding import PartitionSpec as P

ROUNDS = 2
LEARN_RATE = 0.5
MESH = pl.DeviceIdType.MESH
PACK = 16
LANES = 128
DIRECT_MAX = 2
CHUNK = 8
BF = jnp.bfloat16
F32 = jnp.float32


def nt(a, b):
    return lax.dot_general(a, b, (((1,), (1,)), ((), ())), preferred_element_type=F32)


def tn(a, b):
    return lax.dot_general(a, b, (((0,), (0,)), ((), ())), preferred_element_type=F32)


class Item:
    def __init__(self, refs, mask, offset, place):
        self.cur, self.recv, self.got, self.ssem, self.rsem, self.gs, self.gr = refs
        self.mask, self.offset = mask, offset
        self.fixed = mask is not None
        self.dom, self.tile, self.n_dom, self.n_tile = place
        self.stages = 1 if self.fixed else self.n_dom.bit_length() - 1
        self.at = 0
        self.sends = []

    def start(self):
        if self.fixed:
            to = flip_bits(self.dom, self.mask)
        else:
            to = flip_bit(self.dom, self.at)
        self.copy = pltpu.make_async_remote_copy(
            src_ref=self.cur.at[self.at],
            dst_ref=self.recv.at[self.at],
            send_sem=self.ssem.at[self.at],
            recv_sem=self.rsem.at[self.at],
            device_id=(to, self.tile),
            device_id_type=MESH,
        )
        self.copy.start()
        self.sends.append(self.copy)

    def advance(self):
        self.copy.wait_recv()
        if self.fixed:
            final = self.recv.at[0]
        else:
            new = self.recv[self.at].astype(F32)
            old = self.cur[self.at].astype(F32)
            bit = (self.offset >> self.at) & 1
            take = jnp.broadcast_to(bit, new.shape) == 1
            self.cur[self.at + 1] = jnp.where(take, new, old).astype(BF)
            final = self.cur.at[self.at + 1]
        self.at += 1
        if self.at < self.stages:
            self.start()
            return
        self.copies = spread(final, self.got, self.gs, self.gr, self.tile, self.dom, self.n_tile)
        self.sends += self.copies
        self.got[self.tile] = final[...]

    def finish(self):
        while self.at < self.stages:
            self.advance()

    def arrive(self):
        for copy in self.copies:
            copy.wait_recv()


def flip_bit(value, bit):
    step = 1 << bit
    return value + step - 2 * step * lax.rem(lax.div(value, step), 2)


def flip_bits(value, mask):
    other = value
    for bit in range(mask.bit_length()):
        if mask >> bit & 1:
            other = flip_bit(other, bit)
    return other


def spread(src, got, send_sems, recv_sems, tile, dom, n_tile):
    copies = []
    for d in range(1, n_tile):
        copy = pltpu.make_async_remote_copy(
            src_ref=src,
            dst_ref=got.at[tile],
            send_sem=send_sems.at[d - 1],
            recv_sem=recv_sems.at[d - 1],
            device_id=(dom, lax.rem(tile + d, n_tile)),
            device_id_type=MESH,
        )
        copy.start()
        copies.append(copy)
    return copies


def kernel(mask0, mask1, n_dom, n_tile, senders, edges, *refs):
    offs, counts, neg, emb, state, lhs, rhs, out, out_state = refs[:9]
    items = [refs[9 + 7 * i : 16 + 7 * i] for i in range(4)]
    own_got, own_gs, own_gr, group, acc, own_cur = refs[37:]
    dom, tile = lax.axis_index("dom"), lax.axis_index("tile")
    quarter, width = emb.shape
    rows_all = quarter * n_tile
    slots = lhs.shape[1]
    bits = n_dom.bit_length() - 1

    barrier = pltpu.get_barrier_semaphore()
    peers = [(dom, lax.rem(tile + d, n_tile)) for d in range(1, n_tile)]
    if mask0 is None or mask1 is None:
        peers += [(flip_bit(dom, bit), tile) for bit in range(bits)]
    peers += [(flip_bits(dom, mask), tile) for mask in sorted({mask0, mask1} - {None})]
    for peer in peers:
        pl.semaphore_signal(barrier, inc=1, device_id=peer, device_id_type=MESH)

    place = (dom, tile, n_dom, n_tile)
    table0 = Item(items[0], mask0, offs[0], place)
    rows0 = Item(items[1], mask0, offs[0], place)
    rows1 = Item(items[2], mask1, offs[1], place)
    table1 = Item(items[3], mask1, offs[1], place)

    lane = lax.broadcasted_iota(jnp.int32, (1, LANES), 1)
    slot_of = lax.broadcasted_iota(jnp.int32, (slots, edges), 0) + tile * slots
    low = emb[...].astype(BF)
    table0.cur[0] = low
    for rnd in range(ROUNDS):
        alive = slot_of < jnp.broadcast_to(counts[rnd], slot_of.shape)
        left = jnp.where(alive, lhs[rnd].astype(F32), -1.0)
        right = jnp.where(alive, rhs[rnd].astype(F32), -1.0)
        blocks = jnp.zeros((1, LANES), F32)
        for g in range(slots):
            value = jnp.broadcast_to(neg[rnd, g], blocks.shape).astype(F32)
            blocks = jnp.where(lane == tile * slots + g, value, blocks)
        parts = []
        for at in range(0, slots, CHUNK):
            parts += [left[at : at + CHUNK], right[at : at + CHUNK]]
        parts.append(jnp.broadcast_to(blocks, (PACK, LANES)))
        packed = jnp.concatenate(parts, axis=0).astype(BF)
        own_cur[rnd] = packed
        own_got[rnd, tile] = packed
        (rows0 if rnd == 0 else rows1).cur[0] = packed

    pl.semaphore_wait(barrier, len(peers))

    own = []
    rows0.start()
    for rnd in range(ROUNDS):
        own.append(
            spread(
                own_cur.at[rnd], own_got.at[rnd], own_gs.at[rnd], own_gr.at[rnd], tile, dom, n_tile
            )
        )
        (table0 if rnd == 0 else rows1).start()

    chunks = slots // CHUNK
    span = CHUNK * edges
    slot_row = lax.broadcasted_iota(jnp.int32, (LANES, span), 0)
    edge_slot = lax.broadcasted_iota(jnp.int32, (LANES, span), 1) // edges

    def fill(i, carry):
        group[i] = jnp.where(slot_row == edge_slot + i * CHUNK, 1.0, 0.0).astype(BF)
        return carry

    lax.fori_loop(0, senders * chunks, fill, 0)

    key = lax.broadcasted_iota(jnp.int32, (rows_all, edges), 0).astype(F32).astype(BF)
    mine = lax.broadcasted_iota(jnp.int32, (quarter, edges), 0) + tile * quarter
    mine = mine.astype(F32).astype(BF)
    one, zero = jnp.ones((), BF), jnp.zeros((), BF)

    def count(which, got, swap, first, last):
        if first == 0:
            acc[which] = jnp.zeros(acc.shape[1:], F32)

        def body(i, carry):
            s, chunk = lax.div(i, chunks), lax.rem(i, chunks)
            held = got[s, pl.ds(pl.multiple_of(chunk * PACK, PACK), PACK), :]
            keys, mines = [], []
            for g in range(CHUNK):
                src, dst = held[g : g + 1], held[CHUNK + g : CHUNK + g + 1]
                for_mine, for_key = (dst, src) if swap else (src, dst)
                keys.append(jnp.where(key == for_key, one, zero))
                mines.append(jnp.where(mine == for_mine, one, zero))
            pick_mine = jnp.concatenate(mines, axis=1)
            pick = jnp.concatenate([jnp.concatenate(keys, axis=1), pick_mine], axis=0)
            against = jnp.concatenate([group[i], pick_mine], axis=0)
            acc[which] += nt(pick, against)
            return carry

        lax.fori_loop(first * chunks, last * chunks, body, 0)

    def neg_row(got):
        last = slice(chunks * PACK, (chunks + 1) * PACK)
        total = got[0, last].astype(F32)
        for s in range(1, senders):
            total = total + got[s, last].astype(F32)
        return total[:1]

    key_block = (lax.broadcasted_iota(jnp.int32, (rows_all, LANES), 0) // edges).astype(F32)
    mine_block = (
        (lax.broadcasted_iota(jnp.int32, (quarter, LANES), 0) + tile * quarter) // edges
    ).astype(F32)

    def pair_counts(rnd, own_rows, other_rows):
        a, b = 2 * rnd, 2 * rnd + 1
        own_key = acc[a, :rows_all, :LANES] + jnp.where(key_block == neg_row(own_rows), 1.0, 0.0)
        own_mine = acc[a, rows_all:, :LANES]
        other_key = acc[b, :rows_all, :LANES]
        other_mine = acc[b, rows_all:, :LANES] + jnp.where(
            mine_block == neg_row(other_rows), 1.0, 0.0
        )
        every = nt(
            jnp.concatenate([own_key, other_key], axis=1).astype(BF),
            jnp.concatenate([own_mine, other_mine], axis=1).astype(BF),
        )
        positive = acc[a, :rows_all, LANES:] + acc[b, :rows_all, LANES:]
        return every - positive, positive

    eye = lax.broadcasted_iota(jnp.int32, (quarter, quarter), 0) == lax.broadcasted_iota(
        jnp.int32, (quarter, quarter), 1
    )

    def update(low, got, pairs, table, held):
        negative, positive = pairs
        other = jnp.concatenate([got[s] for s in range(n_tile)], axis=0)
        scores = nt(other, low)
        off_coef = (jax.nn.sigmoid(scores) / (2 * edges - 1)).astype(BF).astype(F32)
        on_coef = (-jax.nn.sigmoid(-scores)).astype(BF).astype(F32)
        weight = negative * off_coef + positive * on_coef
        high = weight.astype(BF)
        rest = (weight - high.astype(F32)).astype(BF)
        both = tn(jnp.concatenate([high, rest], axis=1), other)
        total = both[:quarter] + both[quarter:]
        held = held + jnp.sum(total * total, axis=1, keepdims=True) / width
        return table - LEARN_RATE * total / jnp.sqrt(held), held

    most = max(senders - 1, 1)
    for copy in own[0]:
        copy.wait_recv()
    count(0, own_got.at[0], False, 0, senders)
    while table0.at < table0.stages:
        rows0.advance()
        table0.advance()
    rows1.finish()
    for copy in own[1]:
        copy.wait_recv()
    count(2, own_got.at[1], False, 0, most)
    rows0.arrive()
    count(1, rows0.got, True, 0, senders)
    pairs = pair_counts(0, own_got.at[0], rows0.got)
    table0.arrive()
    held = jnp.sum(jnp.where(eye, state[...], 0.0), axis=1, keepdims=True)
    table, held = update(low, table0.got, pairs, emb[...], held)
    low = table.astype(BF)
    table1.cur[0] = low
    out[...] = table
    table1.start()
    count(2, own_got.at[1], False, most, senders)
    rows1.arrive()
    count(3, rows1.got, True, 0, most)
    table1.finish()
    count(3, rows1.got, True, most, senders)
    pairs = pair_counts(1, own_got.at[1], rows1.got)
    table1.arrive()
    table, held = update(table1.cur[0], table1.got, pairs, out[...], held)
    out[...] = table
    out_state[...] = jnp.sum(jnp.where(eye, held, 0.0), axis=0, keepdims=True)
    for copy in table0.sends + rows0.sends + rows1.sends + table1.sends + own[0] + own[1]:
        copy.wait_send()


def shards(n_dom, n_tile, embeddings, adagrad_state, offsets, lhs_rows, rhs_rows, neg_blocks, tile_counts):
    quarter, width = embeddings.shape
    slots, edges = lhs_rows.shape[2], lhs_rows.shape[3]
    rows_all = quarter * n_tile
    bits = n_dom.bit_length() - 1
    senders = (3 * n_tile + 3) // 4
    dma = pltpu.SemaphoreType.DMA

    def item(rows, lanes):
        return [
            pltpu.VMEM((bits + 1, rows, lanes), BF),
            pltpu.VMEM((bits, rows, lanes), BF),
            pltpu.VMEM((n_tile, rows, lanes), BF),
            dma((bits,)),
            dma((bits,)),
            dma((n_tile - 1,)),
            dma((n_tile - 1,)),
        ]

    message = (slots // CHUNK + 1) * PACK
    smem = pl.BlockSpec(memory_space=pltpu.SMEM)
    vmem = pl.BlockSpec(memory_space=pltpu.VMEM)

    def call(mask0, mask1, ident, *args):
        return pl.pallas_call(
            functools.partial(kernel, mask0, mask1, n_dom, n_tile, senders, edges),
            out_shape=(
                jax.ShapeDtypeStruct((quarter, width), F32),
                jax.ShapeDtypeStruct((1, quarter), F32),
            ),
            in_specs=[smem] * 3 + [vmem] * 4,
            out_specs=(vmem, vmem),
            scratch_shapes=item(quarter, width)
            + item(message, LANES)
            + item(message, LANES)
            + item(quarter, width)
            + [
                pltpu.VMEM((ROUNDS, n_tile, message, LANES), BF),
                dma((ROUNDS, n_tile - 1)),
                dma((ROUNDS, n_tile - 1)),
                pltpu.VMEM((senders * slots // CHUNK, LANES, CHUNK * edges), BF),
                pltpu.VMEM((2 * ROUNDS, rows_all + quarter, LANES + quarter), F32),
                pltpu.VMEM((ROUNDS, message, LANES), BF),
            ],
            compiler_params=pltpu.CompilerParams(
                collective_id=ident,
                has_side_effects=True,
                vmem_limit_bytes=40 << 20,
            ),
        )(*args)

    full = n_dom - 1
    if n_dom <= DIRECT_MAX:
        cases = [(full, mask) for mask in range(1, n_dom)]
        cases += [(mask, full) for mask in range(1, full)]
        case = jnp.where(offsets[0] == full, offsets[1] - 1, full + offsets[0] - 1)
    else:
        cases = [(full, None), (None, full)]
        case = jnp.where(offsets[0] == full, 0, 1)
    table, state = lax.switch(
        case,
        [functools.partial(call, *masks, ident) for ident, masks in enumerate(cases)],
        offsets,
        tile_counts[0],
        neg_blocks[0],
        embeddings,
        adagrad_state.reshape(1, quarter),
        lhs_rows[0],
        rhs_rows[0],
    )
    return table, state.reshape(quarter)


def solution(mesh):
    return jax.shard_map(
        functools.partial(shards, mesh.shape["dom"], mesh.shape["tile"]),
        mesh=mesh,
        in_specs=(
            P(("dom", "tile"), None),
            P(("dom", "tile")),
            P(),
            P("dom", None, "tile", None),
            P("dom", None, "tile", None),
            P("dom", None, "tile"),
            P("dom", None),
        ),
        out_specs=(P(("dom", "tile"), None), P(("dom", "tile"))),
        check_vma=False,
    )
```

profile of v0, /device:TPU:0, one launch (start us, length us, event | category | flops | bytes accessed | tf_op | source)
XLA Modules:
  0.0 41.8 jit_solution(7556512238790307232)
XLA Ops:
  0.6 0.0 copy-start.1
  0.6 0.6 %copy-done.1 = s32[2]{0:T(128)S(1)} copy-done((s32[2]{0:T(128)S(1)}, s32[2]{0:T(128)}, u32[]{:S(2)}) %copy-start.1) | copy-done | bytes 32
  1.3 0.0 copy-start.3
  1.3 0.0 copy-start
  1.4 0.0 copy-start.2
  1.4 0.6 %copy-done.3 = f32[64]{0:T(128)S(1)} copy-done((f32[64]{0:T(128)S(1)}, f32[64]{0:T(128)}, u32[]{:S(2)}) %copy-start.3) | copy-done | bytes 280
  2.0 0.0 copy-done
  2.0 0.0 copy-done.2
  2.0 38.6 %conditional.1 = (f32[64,256]{1,0:T(8,128)S(1)}, f32[64]{0:T(128)S(1)}) conditional(s32[]{:T(128)} %bitcast.2, (s32[2]{0:T(128)S(1)}, s32[2]{0:T(128)S(1)}, s32[2,24]{1,0:T(2,128)S(1)}, f32[64,256]{1,0:T(8,128)}, f32[1,64]{1,0:T(1,128)S(1)}, /*index=5*/s32[2,24,128]{2,1,0:T(8,128)}, s32[2,24,128]{2,1,0:T(8,128)}) %tuple.34, (s32[2]{0:T(128)S(1)}, ...), branch_computations={%region_0.1_spmd, %region_1.2_spmd} | conditional | bytes 16 | solution.py:345
  2.0 38.6 %branch_0_fun.1 = (f32[64,256]{1,0:T(8,128)S(1)}, f32[1,64]{1,0:T(1,128)S(1)}) custom-call(s32[2]{0:T(128)S(1)} %get-tuple-element.33.refs_0_, s32[2]{0:T(128)S(1)} %get-tuple-element.34.refs_1_, s32[2,24]{1,0:T(2,128)S(1)} %get-tuple-element.35.refs_2_, f32[64,256]{1,0:T(8,128)} %get-tuple-element.36.refs_3_, f32[1,64]{1,0:T(1,128)S(1)} %get-tuple-element.37.refs_4_, ...), custom_call_target="tpu_custom_call" | custom-call | tf_op jit(solution)/shard_map/cond/branch_0_fun/pallas_call | solution.py:310
  40.6 0.6 %copy.17 = f32[64,256]{1,0:T(8,128)} copy(f32[64,256]{1,0:T(8,128)S(1)} %get-tuple-element.60) | data formatting | bytes 131072
  41.2 0.5 %copy.18 = f32[64]{0:T(128)} copy(f32[64]{0:T(128)S(1)} %get-tuple-element.61) | data formatting | bytes 512
Async XLA Ops:
  0.6 0.7 %copy-start.1 = (s32[2]{0:T(128)S(1)}, s32[2]{0:T(128)}, u32[]{:S(2)}) copy-start(s32[2]{0:T(128)} %param.11) | copy-start | bytes 28
  1.3 0.7 %copy-start.3 = (f32[64]{0:T(128)S(1)}, f32[64]{0:T(128)}, u32[]{:S(2)}) copy-start(f32[64]{0:T(128)} %param.10) | copy-start | bytes 772
  1.3 0.7 %copy-start = (s32[1,2,24]{2,1,0:T(2,128)S(1)}, s32[1,2,24]{2,1,0:T(2,128)}, u32[]{:S(2)}) copy-start(s32[1,2,24]{2,1,0:T(2,128)} %param.14) | copy-start | bytes 580
  1.4 0.7 %copy-start.2 = (s32[1,2]{1,0:T(1,128)S(1)}, s32[1,2]{1,0:T(1,128)}, u32[]{:S(2)}) copy-start(s32[1,2]{1,0:T(1,128)} %param.15) | copy-start | bytes 28
where the time goes:
time: 41.9 us; the launch traced here: 41.8 us
  Pallas kernels  38.6 us (92%)
  local copies, waits for them, and re-layouts  2.47 us (6%)
  between operations  0.72 us (2%)
    pallas_call x1, Pallas kernels, call(): pl.pallas_call(functools.partial(kernel, mask0, mask1, n_dom, n_tile, sen...  38.6 us
    unnamed x10, local copies, waits for them, and re-layouts  2.47 us

commit v1 on v0

--- a/solution.py
+++ b/solution.py
@@ -12,7 +12,7 @@
 MESH = pl.DeviceIdType.MESH
 PACK = 16
 LANES = 128
-DIRECT_MAX = 2
+ALL_MAX = 8
 CHUNK = 8
 BF = jnp.bfloat16
 F32 = jnp.float32
@@ -32,11 +32,30 @@
         self.mask, self.offset = mask, offset
         self.fixed = mask is not None
         self.dom, self.tile, self.n_dom, self.n_tile = place
-        self.stages = 1 if self.fixed else self.n_dom.bit_length() - 1
+        self.to_all = not self.fixed and self.n_dom <= ALL_MAX
+        self.stages = 1 if self.fixed or self.to_all else self.n_dom.bit_length() - 1
         self.at = 0
         self.sends = []
 
+    def start_all(self):
+        self.copies = []
+        for mask in range(1, self.n_dom):
+            copy = pltpu.make_async_remote_copy(
+                src_ref=self.cur.at[0],
+                dst_ref=self.recv.at[mask - 1],
+                send_sem=self.ssem.at[mask - 1],
+                recv_sem=self.rsem.at[mask - 1],
+                device_id=(flip_bits(self.dom, mask), self.tile),
+                device_id_type=MESH,
+            )
+            copy.start()
+            self.copies.append(copy)
+        self.sends += self.copies
+
     def start(self):
+        if self.to_all:
+            self.start_all()
+            return
         if self.fixed:
             to = flip_bits(self.dom, self.mask)
         else:
@@ -53,9 +72,13 @@
         self.sends.append(self.copy)
 
     def advance(self):
-        self.copy.wait_recv()
+        for copy in self.copies if self.to_all else [self.copy]:
+            copy.wait_recv()
         if self.fixed:
             final = self.recv.at[0]
+        elif self.to_all:
+            self.cur[1] = self.recv[jnp.maximum(self.offset - 1, 0)]
+            final = self.cur.at[1]
         else:
             new = self.recv[self.at].astype(F32)
             old = self.cur[self.at].astype(F32)
@@ -122,8 +145,11 @@
     barrier = pltpu.get_barrier_semaphore()
     peers = [(dom, lax.rem(tile + d, n_tile)) for d in range(1, n_tile)]
     if mask0 is None or mask1 is None:
-        peers += [(flip_bit(dom, bit), tile) for bit in range(bits)]
-    peers += [(flip_bits(dom, mask), tile) for mask in sorted({mask0, mask1} - {None})]
+        steps = range(1, n_dom) if n_dom <= ALL_MAX else [1 << bit for bit in range(bits)]
+    else:
+        steps = []
+    steps = sorted(set(steps) | ({mask0, mask1} - {None}))
+    peers += [(flip_bits(dom, mask), tile) for mask in steps]
     for peer in peers:
         pl.semaphore_signal(barrier, inc=1, device_id=peer, device_id_type=MESH)
 
@@ -290,14 +316,15 @@
     bits = n_dom.bit_length() - 1
     senders = (3 * n_tile + 3) // 4
     dma = pltpu.SemaphoreType.DMA
+    arrivals = n_dom - 1 if n_dom <= ALL_MAX else bits
 
     def item(rows, lanes):
         return [
             pltpu.VMEM((bits + 1, rows, lanes), BF),
-            pltpu.VMEM((bits, rows, lanes), BF),
+            pltpu.VMEM((arrivals, rows, lanes), BF),
             pltpu.VMEM((n_tile, rows, lanes), BF),
-            dma((bits,)),
-            dma((bits,)),
+            dma((arrivals,)),
+            dma((arrivals,)),
             dma((n_tile - 1,)),
             dma((n_tile - 1,)),
         ]
@@ -334,17 +361,7 @@
             ),
         )(*args)
 
-    full = n_dom - 1
-    if n_dom <= DIRECT_MAX:
-        cases = [(full, mask) for mask in range(1, n_dom)]
-        cases += [(mask, full) for mask in range(1, full)]
-        case = jnp.where(offsets[0] == full, offsets[1] - 1, full + offsets[0] - 1)
-    else:
-        cases = [(full, None), (None, full)]
-        case = jnp.where(offsets[0] == full, 0, 1)
-    table, state = lax.switch(
-        case,
-        [functools.partial(call, *masks, ident) for ident, masks in enumerate(cases)],
+    operands = (
         offsets,
         tile_counts[0],
         neg_blocks[0],
@@ -353,6 +370,15 @@
         lhs_rows[0],
         rhs_rows[0],
     )
+    if n_dom <= ALL_MAX:
+        table, state = call(None, None, 0, *operands)
+    else:
+        table, state = lax.cond(
+            offsets[0] == n_dom - 1,
+            functools.partial(call, n_dom - 1, None, 0),
+            functools.partial(call, None, n_dom - 1, 1),
+            *operands,
+        )
     return table, state.reshape(quarter)
 
 

time: 41.9 us -> 41.7 us (level)
  Pallas kernels: 38.6 us -> 36.6 us
  local copies, waits for them, and re-layouts: 2.47 us -> 4.14 us
    pallas_call x1, Pallas kernels: 38.6 us -> 36.6 us  [call(): pl.pallas_call(functools.partial(kernel, mask0, mask1, n_dom, n_tile, sen...]
    unnamed x10 -> x16, local copies, waits for them, and re-layouts: 2.47 us -> 4.14 us
where the time goes in v1:
time: 41.7 us; the launch traced here: 41.4 us
  Pallas kernels  36.6 us (88%)
  local copies, waits for them, and re-layouts  4.14 us (10%)
  between operations  0.68 us (2%)
    pallas_call x1, Pallas kernels, call(): pl.pallas_call(functools.partial(kernel, mask0, mask1, n_dom, n_tile, sen...  36.6 us
    unnamed x16, local copies, waits for them, and re-layouts  4.14 us

profile of v1, /device:TPU:0, one launch (start us, length us, event | category | flops | bytes accessed | tf_op | source)
XLA Modules:
  0.0 41.4 jit_solution(15059031082945929758)
XLA Ops:
  0.6 0.0 copy-start.5
  0.6 0.0 copy-start.6
  0.7 0.0 copy-start.3
  0.7 0.0 copy-start.4
  0.7 0.6 %copy-done.5 = s32[1,2]{1,0:T(1,128)S(1)} copy-done((s32[1,2]{1,0:T(1,128)S(1)}, s32[1,2]{1,0:T(1,128)}, u32[]{:S(2)}) %copy-start.5) | copy-done | bytes 32
  1.3 0.0 copy-done.6
  1.3 0.0 copy-done.3
  1.3 0.0 copy-done.4
  1.3 0.0 copy-start
  1.3 0.8 %copy-done = f32[64,256]{1,0:T(8,128)S(1)} copy-done((f32[64,256]{1,0:T(8,128)S(1)}, f32[64,256]{1,0:T(8,128)}, u32[]{:S(2)}) %copy-start) | copy-done | bytes 65560
  2.2 0.0 copy-start.1
  2.2 0.7 %copy-done.1 = s32[1,2,24,128]{3,2,1,0:T(8,128)S(1)} copy-done((s32[1,2,24,128]{3,2,1,0:T(8,128)S(1)}, s32[1,2,24,128]{3,2,1,0:T(8,128)}, u32[]{:S(2)}) %copy-start.1) | copy-done | bytes 24600
  2.9 0.0 copy-start.2
  2.9 0.7 %copy-done.2 = s32[1,2,24,128]{3,2,1,0:T(8,128)S(1)} copy-done((s32[1,2,24,128]{3,2,1,0:T(8,128)S(1)}, s32[1,2,24,128]{3,2,1,0:T(8,128)}, u32[]{:S(2)}) %copy-start.2) | copy-done | bytes 24600
  3.7 36.6 %shard_map.86 = (f32[64,256]{1,0:T(8,128)S(1)}, f32[1,64]{1,0:T(1,128)S(1)}) custom-call(s32[2]{0:T(128)S(1)} %copy-done.4, s32[2]{0:T(128)S(1)} %bitcast.9, s32[2,24]{1,0:T(2,128)S(1)} %bitcast.8, f32[64,256]{1,0:T(8,128)S(1)} %copy-done, f32[1,64]{1,0:T(1,128)S(1)} %bitcast.10, s32[2,24,128]{2,1,0:T(8,128)S(1)} %bitcast.6, s32[2,24,128]{2,1,0:T(8,128)S(1)} %bitcast.7), custom_call_target="tpu_custom_call" | custom-call | tf_op jit(solution)/shard_map/pallas_call | solution.py:337
  40.3 0.6 %copy.11 = f32[64,256]{1,0:T(8,128)} copy(f32[64,256]{1,0:T(8,128)S(1)} %get-tuple-element.8) | data formatting | bytes 131072
  40.9 0.5 %copy.12 = f32[64]{0:T(128)} copy(f32[64]{0:T(128)S(1)} %bitcast.11) | data formatting | bytes 512
Async XLA Ops:
  0.6 0.7 %copy-start.5 = (s32[1,2]{1,0:T(1,128)S(1)}, s32[1,2]{1,0:T(1,128)}, u32[]{:S(2)}) copy-start(s32[1,2]{1,0:T(1,128)} %param.13) | copy-start | bytes 28
  0.6 0.7 %copy-start.6 = (f32[64]{0:T(128)S(1)}, f32[64]{0:T(128)}, u32[]{:S(2)}) copy-start(f32[64]{0:T(128)} %param.8) | copy-start | bytes 772
  0.7 0.7 %copy-start.3 = (s32[1,2,24]{2,1,0:T(2,128)S(1)}, s32[1,2,24]{2,1,0:T(2,128)}, u32[]{:S(2)}) copy-start(s32[1,2,24]{2,1,0:T(2,128)} %param.12) | copy-start | bytes 580
  0.7 0.7 %copy-start.4 = (s32[2]{0:T(128)S(1)}, s32[2]{0:T(128)}, u32[]{:S(2)}) copy-start(s32[2]{0:T(128)} %refs_0_.1) | copy-start | bytes 28
  1.3 0.8 %copy-start = (f32[64,256]{1,0:T(8,128)S(1)}, f32[64,256]{1,0:T(8,128)}, u32[]{:S(2)}) copy-start(f32[64,256]{1,0:T(8,128)} %refs_3_.1) | copy-start | bytes 196612
  2.2 0.7 %copy-start.1 = (s32[1,2,24,128]{3,2,1,0:T(8,128)S(1)}, s32[1,2,24,128]{3,2,1,0:T(8,128)}, u32[]{:S(2)}) copy-start(s32[1,2,24,128]{3,2,1,0:T(8,128)} %param.10) | copy-start | bytes 73732
  2.9 0.7 %copy-start.2 = (s32[1,2,24,128]{3,2,1,0:T(8,128)S(1)}, s32[1,2,24,128]{3,2,1,0:T(8,128)}, u32[]{:S(2)}) copy-start(s32[1,2,24,128]{3,2,1,0:T(8,128)} %param.11) | copy-start | bytes 73732
